TPU v7x, 128 devices: a whole 4x4x4 slice. The times are simulated.
128 devices in a mesh: blk: 16 (over z, y_lo, core), aux: 8 (over y_hi, x).
Axes of the slice: x: 4, y: 4 (y_hi: 2, y_lo: 2; y = y_hi * 2 + y_lo), z: 4, core: 2. Of those that a mesh axis runs over, the one named last changes fastest.
Arguments:
- coeffs: float32 [2048, 256], P('blk'), may hold values from -6 to 6
- integrals: float32 [16, 128, 128, 16, 128], P('blk', 'aux'), may hold values from -0.01953125 to 0.01953125
- metric: float32 [128, 128], replicated, as said below
- pair_blocks: int32 [16, 16], P('blk'), may hold values from 0 to 15, as said below
- support: int32 [256, 4], replicated, may hold values from 0 to 15, as said below
Outputs:
- exchange_band: float32 [2048, 128], P(('blk', 'aux'))
Inputs may be any that keep to these rules, and one draw needn't show every extreme that they name: `pair_blocks`: each row lists 16 distinct blocks, and row r lists block r first. `support`: each orbital lists 4 distinct blocks. `metric`: symmetric.
All inputs are finite; a program needn't handle non-finite values.
Results may differ from a plain program's by a relative error of at most 0.000061.
Values sent between devices are 32-bit elements; how exact they have to be, the bound alone decides.
A program may use at most 128 MiB of HBM per device.

v0:
```python
import jax
import jax.numpy as jnp
from jax import lax
from jax.sharding import PartitionSpec as P

S = 128
BLOCKS_DEV = 1
PAIRS = 16
NOCC = 256


def from_behind(block, axis, distance):
    devices = range(lax.axis_size(axis))
    route = [((i - distance) % len(devices), i) for i in devices]
    return lax.ppermute(block, axis, route)


def local(coeffs, integrals, metric, pair_blocks, support):
    hi = lax.Precision.HIGHEST
    nblk_axis = lax.axis_size("blk")
    me_blk = lax.axis_index("blk")
    local_ids = me_blk * BLOCKS_DEV + jnp.arange(BLOCKS_DEV, dtype=jnp.int32)
    hit = jnp.any(support[:, :, None] == local_ids[None, None, :], axis=1)
    masked = (
        coeffs.reshape(BLOCKS_DEV, S, NOCC) * jnp.transpose(hit).astype(jnp.float32)[:, None, :]
    )

    def pick(collected, visiting, owner):
        ids = owner * BLOCKS_DEV + jnp.arange(BLOCKS_DEV, dtype=jnp.int32)
        onehot = (pair_blocks[:, :, None] == ids[None, None, :]).astype(jnp.float32)
        return collected + jnp.einsum("bpc,csi->bpsi", onehot, visiting, precision=hi)

    empty = jnp.zeros((BLOCKS_DEV, PAIRS, S, NOCC), jnp.float32)
    first = pick(empty, masked, me_blk)

    def turn(step, carry):
        collected, visiting = carry
        visiting = from_behind(visiting, "blk", 1)
        owner = (me_blk - step) % nblk_axis
        return (pick(collected, visiting, owner), visiting)

    paired, last_seen = lax.fori_loop(1, nblk_axis, turn, (first, masked))
    share = integrals.shape[1]
    half = jnp.einsum(
        "bxk,bki->bxi",
        integrals.reshape(BLOCKS_DEV, share * S, PAIRS * S),
        paired.reshape(BLOCKS_DEV, PAIRS * S, NOCC),
        precision=hi,
    )
    half = half.reshape(BLOCKS_DEV, share, S, NOCC)
    regrouped = lax.all_to_all(half, "aux", split_axis=3, concat_axis=1, tiled=True)
    fitted = jnp.einsum("pq,bqmi->bpmi", metric, regrouped, precision=hi)
    partial_band = jnp.einsum("bpmi,cpni->bmcn", regrouped, fitted, precision=hi)
    partial_band = partial_band.reshape(BLOCKS_DEV * S, BLOCKS_DEV * S)
    return lax.psum_scatter(partial_band, "aux", scatter_dimension=0, tiled=True)


def solution(mesh):
    return jax.shard_map(
        local,
        mesh=mesh,
        in_specs=(P("blk", None), P("blk", "aux", None, None, None), P(), P("blk", None), P()),
        out_specs=P(("blk", "aux"), None),
        check_vma=False,
    )
```

profile of v0, /device:TPU:0, one launch (start us, length us, event | category | flops | bytes accessed | tf_op | source)
XLA Modules:
  0.0 268.5 jit_solution(17779626999344266675)
XLA Ops:
  6.5 0.7 compare_reduce_fusion
  7.3 0.9 fusion.18
  8.2 0.9 broadcast_multiply_fusion
  9.1 0.7 fusion.15
  9.8 0.2 multiply_bitcast_fusion
  10.1 106.9 %while.17 = (s32[]{:T(128)}, f32[1,16,128,256]{3,2,1,0:T(8,128)S(1)}, f32[1,128,256]{2,1,0:T(8,128)S(1)}, s32[]{:T(128)}, s32[1,16]{1,0:T(1,128)S(1)}, /*index=5*/s32[]{:T(128)}, s32[]{:T(128)}, s32[]{:T(128)}, s32[]{:T(128)}) while((s32[]{:T(128)}, f32[1,16,128,256]{3,2,1,0:T(8,128)S(1)}, f32[1,128,256]{2,1,0:T(8,128)S(1)}, s32[]{:T(128)}, ...), condition=%wide.region_2.3_spmd, body=%wide.region_1.2_spmd.sunk | while | flops 1048622 | bytes 5112258 | solution.py:42
  10.1 0.1 collective-permute-start
  10.2 7.2 %collective-permute-done = f32[1,128,256]{2,1,0:T(8,128)S(1)} collective-permute-done((f32[1,128,256]{2,1,0:T(8,128)S(1)}, f32[1,128,256]{2,1,0:T(8,128)S(1)}, u32[]{:S(2)}, u32[]{:S(2)}) %collective-permute-start) | collective-permute-done | bytes 131104 | tf_op jit(solution)/shard_map/while/body/eval_jaxpr/ppermute | solution.py:15
  17.4 0.5 bitcast_add_fusion.2
  17.9 0.1 collective-permute-start
  18.0 6.5 %collective-permute-done = f32[1,128,256]{2,1,0:T(8,128)S(1)} collective-permute-done((f32[1,128,256]{2,1,0:T(8,128)S(1)}, f32[1,128,256]{2,1,0:T(8,128)S(1)}, u32[]{:S(2)}, u32[]{:S(2)}) %collective-permute-start) | collective-permute-done | bytes 131104 | tf_op jit(solution)/shard_map/while/body/eval_jaxpr/ppermute | solution.py:15
  24.4 0.5 bitcast_add_fusion.2
  25.1 6.5 %collective-permute-done = f32[1,128,256]{2,1,0:T(8,128)S(1)} collective-permute-done((f32[1,128,256]{2,1,0:T(8,128)S(1)}, f32[1,128,256]{2,1,0:T(8,128)S(1)}, u32[]{:S(2)}, u32[]{:S(2)}) %collective-permute-start) | collective-permute-done | bytes 131104 | tf_op jit(solution)/shard_map/while/body/eval_jaxpr/ppermute | solution.py:15
  31.5 0.5 bitcast_add_fusion.2
  32.0 0.1 collective-permute-start
  32.1 6.5 %collective-permute-done = f32[1,128,256]{2,1,0:T(8,128)S(1)} collective-permute-done((f32[1,128,256]{2,1,0:T(8,128)S(1)}, f32[1,128,256]{2,1,0:T(8,128)S(1)}, u32[]{:S(2)}, u32[]{:S(2)}) %collective-permute-start) | collective-permute-done | bytes 131104 | tf_op jit(solution)/shard_map/while/body/eval_jaxpr/ppermute | solution.py:15
  38.6 0.5 bitcast_add_fusion.2
  39.2 6.5 %collective-permute-done = f32[1,128,256]{2,1,0:T(8,128)S(1)} collective-permute-done((f32[1,128,256]{2,1,0:T(8,128)S(1)}, f32[1,128,256]{2,1,0:T(8,128)S(1)}, u32[]{:S(2)}, u32[]{:S(2)}) %collective-permute-start) | collective-permute-done | bytes 131104 | tf_op jit(solution)/shard_map/while/body/eval_jaxpr/ppermute | solution.py:15
  45.7 0.5 bitcast_add_fusion.2
  46.3 6.5 %collective-permute-done = f32[1,128,256]{2,1,0:T(8,128)S(1)} collective-permute-done((f32[1,128,256]{2,1,0:T(8,128)S(1)}, f32[1,128,256]{2,1,0:T(8,128)S(1)}, u32[]{:S(2)}, u32[]{:S(2)}) %collective-permute-start) | collective-permute-done | bytes 131104 | tf_op jit(solution)/shard_map/while/body/eval_jaxpr/ppermute | solution.py:15
  52.8 0.5 bitcast_add_fusion.2
  53.4 6.5 %collective-permute-done = f32[1,128,256]{2,1,0:T(8,128)S(1)} collective-permute-done((f32[1,128,256]{2,1,0:T(8,128)S(1)}, f32[1,128,256]{2,1,0:T(8,128)S(1)}, u32[]{:S(2)}, u32[]{:S(2)}) %collective-permute-start) | collective-permute-done | bytes 131104 | tf_op jit(solution)/shard_map/while/body/eval_jaxpr/ppermute | solution.py:15
  59.8 0.5 bitcast_add_fusion.2
  60.5 6.5 %collective-permute-done = f32[1,128,256]{2,1,0:T(8,128)S(1)} collective-permute-done((f32[1,128,256]{2,1,0:T(8,128)S(1)}, f32[1,128,256]{2,1,0:T(8,128)S(1)}, u32[]{:S(2)}, u32[]{:S(2)}) %collective-permute-start) | collective-permute-done | bytes 131104 | tf_op jit(solution)/shard_map/while/body/eval_jaxpr/ppermute | solution.py:15
  66.9 0.5 bitcast_add_fusion.2
  67.5 6.5 %collective-permute-done = f32[1,128,256]{2,1,0:T(8,128)S(1)} collective-permute-done((f32[1,128,256]{2,1,0:T(8,128)S(1)}, f32[1,128,256]{2,1,0:T(8,128)S(1)}, u32[]{:S(2)}, u32[]{:S(2)}) %collective-permute-start) | collective-permute-done | bytes 131104 | tf_op jit(solution)/shard_map/while/body/eval_jaxpr/ppermute | solution.py:15
  74.0 0.5 bitcast_add_fusion.2
  74.6 6.5 %collective-permute-done = f32[1,128,256]{2,1,0:T(8,128)S(1)} collective-permute-done((f32[1,128,256]{2,1,0:T(8,128)S(1)}, f32[1,128,256]{2,1,0:T(8,128)S(1)}, u32[]{:S(2)}, u32[]{:S(2)}) %collective-permute-start) | collective-permute-done | bytes 131104 | tf_op jit(solution)/shard_map/while/body/eval_jaxpr/ppermute | solution.py:15
  81.1 0.5 bitcast_add_fusion.2
  81.7 6.5 %collective-permute-done = f32[1,128,256]{2,1,0:T(8,128)S(1)} collective-permute-done((f32[1,128,256]{2,1,0:T(8,128)S(1)}, f32[1,128,256]{2,1,0:T(8,128)S(1)}, u32[]{:S(2)}, u32[]{:S(2)}) %collective-permute-start) | collective-permute-done | bytes 131104 | tf_op jit(solution)/shard_map/while/body/eval_jaxpr/ppermute | solution.py:15
  88.1 0.5 bitcast_add_fusion.2
  88.8 6.5 %collective-permute-done = f32[1,128,256]{2,1,0:T(8,128)S(1)} collective-permute-done((f32[1,128,256]{2,1,0:T(8,128)S(1)}, f32[1,128,256]{2,1,0:T(8,128)S(1)}, u32[]{:S(2)}, u32[]{:S(2)}) %collective-permute-start) | collective-permute-done | bytes 131104 | tf_op jit(solution)/shard_map/while/body/eval_jaxpr/ppermute | solution.py:15
  95.2 0.5 bitcast_add_fusion.2
  95.8 6.5 %collective-permute-done = f32[1,128,256]{2,1,0:T(8,128)S(1)} collective-permute-done((f32[1,128,256]{2,1,0:T(8,128)S(1)}, f32[1,128,256]{2,1,0:T(8,128)S(1)}, u32[]{:S(2)}, u32[]{:S(2)}) %collective-permute-start) | collective-permute-done | bytes 131104 | tf_op jit(solution)/shard_map/while/body/eval_jaxpr/ppermute | solution.py:15
  102.3 0.5 bitcast_add_fusion.2
  102.9 6.5 %collective-permute-done = f32[1,128,256]{2,1,0:T(8,128)S(1)} collective-permute-done((f32[1,128,256]{2,1,0:T(8,128)S(1)}, f32[1,128,256]{2,1,0:T(8,128)S(1)}, u32[]{:S(2)}, u32[]{:S(2)}) %collective-permute-start) | collective-permute-done | bytes 131104 | tf_op jit(solution)/shard_map/while/body/eval_jaxpr/ppermute | solution.py:15
  109.4 0.5 bitcast_add_fusion.2
  110.0 6.5 %collective-permute-done = f32[1,128,256]{2,1,0:T(8,128)S(1)} collective-permute-done((f32[1,128,256]{2,1,0:T(8,128)S(1)}, f32[1,128,256]{2,1,0:T(8,128)S(1)}, u32[]{:S(2)}, u32[]{:S(2)}) %collective-permute-start) | collective-permute-done | bytes 131104 | tf_op jit(solution)/shard_map/while/body/eval_jaxpr/ppermute | solution.py:15
  116.4 0.5 bitcast_add_fusion.2
  116.9 33.9 %fusion.9 = f32[1,16,128,256]{2,3,1,0:T(8,128)S(1)} fusion(f32[16,128,16,128]{3,2,1,0:T(8,128)} %bitcast.51, f32[1,16,128,256]{3,2,1,0:T(8,128)S(1)} %get-tuple-element.138), kind=kOutput, calls=%fused_computation.10 | convolution fusion | flops 12884901888 | bytes 20971520 | tf_op jit(solution)/shard_map/bxk,bki->bxi/dot_general | solution.py:44
  150.8 1.2 copy.23
  152.1 29.9 %all_to_all.15 = f32[1,16,128,256]{2,1,0,3:T(8,128)S(1)} all-to-all(f32[1,16,128,256]{2,1,0,3:T(8,128)S(1)} %copy.23), channel_id=1, replica_groups=mesh['blk'=16,'aux'=8] {'aux'}, dimensions={3} | all-to-all | bytes 4194304 | tf_op jit(solution)/shard_map/all_to_all | solution.py:51
  182.0 0.7 copy.24
  182.6 0.2 copy.25
  182.9 5.6 %fusion.6 = f32[128,128,32]{0,1,2:T(8,128)} fusion(f32[128,128,32]{1,2,0:T(8,128)S(1)} %bitcast.49, f32[128,128]{1,0:T(8,128)S(1)} %copy-done), kind=kOutput, calls=%fused_computation.9 | convolution fusion | flops 805306368 | bytes 4259840 | tf_op jit(solution)/shard_map/pq,bqmi->bpmi/dot_general | solution.py:52
  188.4 3.1 %copy.27 = f32[128,128,32]{1,2,0:T(8,128)} copy(f32[128,128,32]{0,1,2:T(8,128)} %fusion.6) | data formatting | bytes 4194304 | tf_op jit(solution)/shard_map/reshape.18
  191.5 5.7 %convolution_bitcast_fusion = f32[128,128]{1,0:T(8,128)} fusion(f32[128,128,32]{1,2,0:T(8,128)S(1)} %bitcast.50, f32[128,128,32]{1,2,0:T(8,128)} %copy.27), kind=kOutput, calls=%fused_computation.11 | convolution fusion | flops 805306368 | bytes 4259840 | tf_op jit(solution)/shard_map/bpmi,cpni->bmcn/dot_general | solution.py:53
  197.2 64.4 %reduce-scatter.2.cloned.1.call-done = f32[16,128]{1,0:T(8,128)} async-done(((f32[128,128]{1,0:T(8,128)}), f32[16,128]{1,0:T(8,128)}) %reduce-scatter.2.cloned.1.call-update) | async-done | bytes 8208 | tf_op jit(solution)/shard_map/reduce_scatter | solution.py:55
  (49 shorter events, 1.2 us)
Async XLA Ops:
  6.5 176.3 %copy-start = (f32[128,128]{1,0:T(8,128)S(1)}, f32[128,128]{1,0:T(8,128)}, u32[]{:S(2)}) copy-start(f32[128,128]{1,0:T(8,128)} %param.9) | copy-start | bytes 196612
  6.5 3.5 %copy-start.1 = (s32[1,16]{1,0:T(1,128)S(1)}, s32[1,16]{1,0:T(1,128)}, u32[]{:S(2)}) copy-start(s32[1,16]{1,0:T(1,128)} %param.10) | copy-start | bytes 196
  6.5 255.1 %reduce-scatter.2.cloned.1.call-start = ((), (), s32[]{:S(2)}) async-start(), calls=%async_computation.2 | async-start | bytes 73728 | tf_op jit(solution)/shard_map/reduce_scatter | solution.py:55
  10.1 7.3 %collective-permute-start = (f32[1,128,256]{2,1,0:T(8,128)S(1)}, f32[1,128,256]{2,1,0:T(8,128)S(1)}, u32[]{:S(2)}, u32[]{:S(2)}) collective-permute-start(f32[1,128,256]{2,1,0:T(8,128)S(1)} %get-tuple-element.191), channel_id=1, source_target_pairs={{120,0},{0,8},{8,16},{16,24},{24,32},{32,40},{40,48},{48,56},{56,6... | collective-permute-start | bytes 393224 | tf_op jit(solution)/shard_map/while/body/eval_jaxpr/ppermute | solution.py:15
  17.9 6.6 %collective-permute-start = (f32[1,128,256]{2,1,0:T(8,128)S(1)}, f32[1,128,256]{2,1,0:T(8,128)S(1)}, u32[]{:S(2)}, u32[]{:S(2)}) collective-permute-start(f32[1,128,256]{2,1,0:T(8,128)S(1)} %get-tuple-element.191), channel_id=1, source_target_pairs={{120,0},{0,8},{8,16},{16,24},{24,32},{32,40},{40,48},{48,56},{56,6... | collective-permute-start | bytes 393224 | tf_op jit(solution)/shard_map/while/body/eval_jaxpr/ppermute | solution.py:15
  25.0 6.6 %collective-permute-start = (f32[1,128,256]{2,1,0:T(8,128)S(1)}, f32[1,128,256]{2,1,0:T(8,128)S(1)}, u32[]{:S(2)}, u32[]{:S(2)}) collective-permute-start(f32[1,128,256]{2,1,0:T(8,128)S(1)} %get-tuple-element.191), channel_id=1, source_target_pairs={{120,0},{0,8},{8,16},{16,24},{24,32},{32,40},{40,48},{48,56},{56,6... | collective-permute-start | bytes 393224 | tf_op jit(solution)/shard_map/while/body/eval_jaxpr/ppermute | solution.py:15
  32.0 6.6 %collective-permute-start = (f32[1,128,256]{2,1,0:T(8,128)S(1)}, f32[1,128,256]{2,1,0:T(8,128)S(1)}, u32[]{:S(2)}, u32[]{:S(2)}) collective-permute-start(f32[1,128,256]{2,1,0:T(8,128)S(1)} %get-tuple-element.191), channel_id=1, source_target_pairs={{120,0},{0,8},{8,16},{16,24},{24,32},{32,40},{40,48},{48,56},{56,6... | collective-permute-start | bytes 393224 | tf_op jit(solution)/shard_map/while/body/eval_jaxpr/ppermute | solution.py:15
  39.1 6.6 %collective-permute-start = (f32[1,128,256]{2,1,0:T(8,128)S(1)}, f32[1,128,256]{2,1,0:T(8,128)S(1)}, u32[]{:S(2)}, u32[]{:S(2)}) collective-permute-start(f32[1,128,256]{2,1,0:T(8,128)S(1)} %get-tuple-element.191), channel_id=1, source_target_pairs={{120,0},{0,8},{8,16},{16,24},{24,32},{32,40},{40,48},{48,56},{56,6... | collective-permute-start | bytes 393224 | tf_op jit(solution)/shard_map/while/body/eval_jaxpr/ppermute | solution.py:15
  46.2 6.6 %collective-permute-start = (f32[1,128,256]{2,1,0:T(8,128)S(1)}, f32[1,128,256]{2,1,0:T(8,128)S(1)}, u32[]{:S(2)}, u32[]{:S(2)}) collective-permute-start(f32[1,128,256]{2,1,0:T(8,128)S(1)} %get-tuple-element.191), channel_id=1, source_target_pairs={{120,0},{0,8},{8,16},{16,24},{24,32},{32,40},{40,48},{48,56},{56,6... | collective-permute-start | bytes 393224 | tf_op jit(solution)/shard_map/while/body/eval_jaxpr/ppermute | solution.py:15
  53.3 6.6 %collective-permute-start = (f32[1,128,256]{2,1,0:T(8,128)S(1)}, f32[1,128,256]{2,1,0:T(8,128)S(1)}, u32[]{:S(2)}, u32[]{:S(2)}) collective-permute-start(f32[1,128,256]{2,1,0:T(8,128)S(1)} %get-tuple-element.191), channel_id=1, source_target_pairs={{120,0},{0,8},{8,16},{16,24},{24,32},{32,40},{40,48},{48,56},{56,6... | collective-permute-start | bytes 393224 | tf_op jit(solution)/shard_map/while/body/eval_jaxpr/ppermute | solution.py:15
  60.3 6.6 %collective-permute-start = (f32[1,128,256]{2,1,0:T(8,128)S(1)}, f32[1,128,256]{2,1,0:T(8,128)S(1)}, u32[]{:S(2)}, u32[]{:S(2)}) collective-permute-start(f32[1,128,256]{2,1,0:T(8,128)S(1)} %get-tuple-element.191), channel_id=1, source_target_pairs={{120,0},{0,8},{8,16},{16,24},{24,32},{32,40},{40,48},{48,56},{56,6... | collective-permute-start | bytes 393224 | tf_op jit(solution)/shard_map/while/body/eval_jaxpr/ppermute | solution.py:15
  67.4 6.6 %collective-permute-start = (f32[1,128,256]{2,1,0:T(8,128)S(1)}, f32[1,128,256]{2,1,0:T(8,128)S(1)}, u32[]{:S(2)}, u32[]{:S(2)}) collective-permute-start(f32[1,128,256]{2,1,0:T(8,128)S(1)} %get-tuple-element.191), channel_id=1, source_target_pairs={{120,0},{0,8},{8,16},{16,24},{24,32},{32,40},{40,48},{48,56},{56,6... | collective-permute-start | bytes 393224 | tf_op jit(solution)/shard_map/while/body/eval_jaxpr/ppermute | solution.py:15
  74.5 6.6 %collective-permute-start = (f32[1,128,256]{2,1,0:T(8,128)S(1)}, f32[1,128,256]{2,1,0:T(8,128)S(1)}, u32[]{:S(2)}, u32[]{:S(2)}) collective-permute-start(f32[1,128,256]{2,1,0:T(8,128)S(1)} %get-tuple-element.191), channel_id=1, source_target_pairs={{120,0},{0,8},{8,16},{16,24},{24,32},{32,40},{40,48},{48,56},{56,6... | collective-permute-start | bytes 393224 | tf_op jit(solution)/shard_map/while/body/eval_jaxpr/ppermute | solution.py:15
  81.6 6.6 %collective-permute-start = (f32[1,128,256]{2,1,0:T(8,128)S(1)}, f32[1,128,256]{2,1,0:T(8,128)S(1)}, u32[]{:S(2)}, u32[]{:S(2)}) collective-permute-start(f32[1,128,256]{2,1,0:T(8,128)S(1)} %get-tuple-element.191), channel_id=1, source_target_pairs={{120,0},{0,8},{8,16},{16,24},{24,32},{32,40},{40,48},{48,56},{56,6... | collective-permute-start | bytes 393224 | tf_op jit(solution)/shard_map/while/body/eval_jaxpr/ppermute | solution.py:15
  88.6 6.6 %collective-permute-start = (f32[1,128,256]{2,1,0:T(8,128)S(1)}, f32[1,128,256]{2,1,0:T(8,128)S(1)}, u32[]{:S(2)}, u32[]{:S(2)}) collective-permute-start(f32[1,128,256]{2,1,0:T(8,128)S(1)} %get-tuple-element.191), channel_id=1, source_target_pairs={{120,0},{0,8},{8,16},{16,24},{24,32},{32,40},{40,48},{48,56},{56,6... | collective-permute-start | bytes 393224 | tf_op jit(solution)/shard_map/while/body/eval_jaxpr/ppermute | solution.py:15
  95.7 6.6 %collective-permute-start = (f32[1,128,256]{2,1,0:T(8,128)S(1)}, f32[1,128,256]{2,1,0:T(8,128)S(1)}, u32[]{:S(2)}, u32[]{:S(2)}) collective-permute-start(f32[1,128,256]{2,1,0:T(8,128)S(1)} %get-tuple-element.191), channel_id=1, source_target_pairs={{120,0},{0,8},{8,16},{16,24},{24,32},{32,40},{40,48},{48,56},{56,6... | collective-permute-start | bytes 393224 | tf_op jit(solution)/shard_map/while/body/eval_jaxpr/ppermute | solution.py:15
  102.8 6.6 %collective-permute-start = (f32[1,128,256]{2,1,0:T(8,128)S(1)}, f32[1,128,256]{2,1,0:T(8,128)S(1)}, u32[]{:S(2)}, u32[]{:S(2)}) collective-permute-start(f32[1,128,256]{2,1,0:T(8,128)S(1)} %get-tuple-element.191), channel_id=1, source_target_pairs={{120,0},{0,8},{8,16},{16,24},{24,32},{32,40},{40,48},{48,56},{56,6... | collective-permute-start | bytes 393224 | tf_op jit(solution)/shard_map/while/body/eval_jaxpr/ppermute | solution.py:15
  109.9 6.6 %collective-permute-start = (f32[1,128,256]{2,1,0:T(8,128)S(1)}, f32[1,128,256]{2,1,0:T(8,128)S(1)}, u32[]{:S(2)}, u32[]{:S(2)}) collective-permute-start(f32[1,128,256]{2,1,0:T(8,128)S(1)} %get-tuple-element.191), channel_id=1, source_target_pairs={{120,0},{0,8},{8,16},{16,24},{24,32},{32,40},{40,48},{48,56},{56,6... | collective-permute-start | bytes 393224 | tf_op jit(solution)/shard_map/while/body/eval_jaxpr/ppermute | solution.py:15
Sparse Core Ops, SparseCore 0:
  197.3 64.2 reduce-scatter.1
where the time goes:
time: 269 us; the launch traced here: 268 us
  waiting for transfers between devices  162 us (60%)
  matrix products  45.1 us (17%)
  blocking collectives  29.9 us (11%)
  between operations  13.5 us (5%)
  other arithmetic  10.6 us (4%)
  local copies, waits for them, and re-layouts  5.38 us (2%)
    ppermute x15, waiting for transfers between devices, from_behind(): return lax.ppermute(block, axis, route)  97.6 us
    reduce_scatter x1, waiting for transfers between devices, local(): lax.psum_scatter(partial_band, 'aux', scatter_dimension=0, tiled=True)  64.4 us
    dot_general x1, matrix products, local(): jnp.einsum('bxk,bki->bxi', integrals.reshape(BLOCKS_DEV, share * S, PAIRS...  33.9 us
    all_to_all x1, blocking collectives, local(): lax.all_to_all(half, 'aux', split_axis=3, concat_axis=1, tiled=True)  29.9 us
    add x15, other arithmetic, pick(): collected + jnp.einsum('bpc,csi->bpsi', onehot, visiting, precision=hi)  7.01 us
    dot_general x1, matrix products, local(): jnp.einsum('bpmi,cpni->bmcn', regrouped, fitted, precision=hi)  5.66 us
    dot_general x1, matrix products, local(): fitted = jnp.einsum('pq,bqmi->bpmi', metric, regrouped, precision=hi)  5.55 us
  transfers between devices with their start and end apart: 16, of which 16 were waited for; matrix products, arithmetic and copies ran while one was open for 0% of the time, Pallas kernels for 0%

commit v1 on v0

v1 whole, which is shorter than its diff:
```python
import functools

import jax
import jax.numpy as jnp
from jax import lax
from jax.experimental import pallas as pl
from jax.experimental.pallas import tpu as pltpu
from jax.sharding import PartitionSpec as P

S = 128
PAIRS = 16
NOCC = 256
SHARE = 16
NAUX = 128
K = PAIRS * S
QROWS = 64
CHUNKS = ((0, 64), (64, 64), (128, 128))
NGROUPS = 8
f32, bf16 = jnp.float32, jnp.bfloat16
MESH = pl.DeviceIdType.MESH
NN = (((1,), (0,)), ((), ()))
NT = (((1,), (1,)), ((), ()))
PEERS = [(dx, dy) for dy in (1, 0) for dx in (2, 1, 3, 0) if (dx, dy) != (0, 0)]
GATHER = [(1, 2), (1, 1), (1, 3), (0, 2), (0, 1), (0, 3), (1, 0)]


def split(v):
    hi = v.astype(bf16)
    return hi, (v - hi.astype(f32)).astype(bf16)


def dot3(a, b, dims=NN):
    ah, al = a
    bh, bl = b
    d = functools.partial(lax.dot_general, dimension_numbers=dims, preferred_element_type=f32)
    return d(ah, bh) + (d(ah, bl) + d(al, bh))


def kernel(
    pair_ref, coeffs_hbm, support_hbm, metric_hbm, ints_ref, out_ref,
    coeffs_ref, support_ref, metric_ref, ints, i_hi, i_lo, ct0, ct1, ct2, lhs0, lhs1, lhs01, lhs2, half01, half23, recv01, recv23, band, bands,
    in_sem, i_sem, g_send, g_recv, y_send, y_recv, z_send, z_recv, c_send, c_recv, a_send, a_recv, b_send, b_recv,
):
    blk, aux = lax.axis_index("blk"), lax.axis_index("aux")
    core, ylo, z = lax.rem(blk, 2), lax.rem(blk // 2, 2), blk // 4
    x, yhi = lax.rem(aux, 4), aux // 4
    y = yhi * 2 + ylo
    zy = z * 2 + ylo
    cts = (ct0, ct1, ct2)

    def device(x, y, z, core):
        return ((z * 2 + lax.rem(y, 2)) * 2 + core, (y // 2) * 4 + x)

    def aux_peer(dx, dy):
        return lax.rem(yhi + dy, 2) * 4 + lax.rem(x + dx, 4)

    def gather_peer(oy, dz, sign):
        step = oy * (1 + 2 * core) if sign > 0 else oy * (3 - 2 * core)
        return device(x, lax.rem(y + step, 4), lax.rem(z + (dz if sign > 0 else 4 - dz), 4), core)

    sibling = (blk + 1 - 2 * core, aux)

    inputs = []
    for i, (src, dst) in enumerate(
        ((coeffs_hbm, coeffs_ref), (support_hbm, support_ref), (metric_hbm, metric_ref))
    ):
        load = pltpu.make_async_copy(src, dst, in_sem.at[i])
        load.start()
        inputs.append(load)
    barrier = pltpu.get_barrier_semaphore()
    for oy, dz in GATHER:
        pl.semaphore_signal(barrier, inc=1, device_id=gather_peer(oy, dz, -1), device_id_type=MESH)
    for dx, dy in PEERS:
        pl.semaphore_signal(barrier, inc=1, device_id=(blk, aux_peer(dx, dy)), device_id_type=MESH)
    pl.semaphore_signal(barrier, inc=1, device_id=sibling, device_id_type=MESH)

    inputs[0].wait()
    inputs[1].wait()
    loads = []
    rows = SHARE * S * PAIRS // NGROUPS
    for g in range(NGROUPS):
        load = pltpu.make_async_copy(
            ints_ref.at[pl.ds(g * rows, rows)], ints.at[pl.ds(g * rows, rows)], i_sem.at[g]
        )
        load.start()
        loads.append(load)

    hit = jnp.max((support_ref[...] == blk).astype(f32), axis=0, keepdims=True)
    masked = (coeffs_ref[...] * hit).T
    for ct, (first, n) in zip(cts, CHUNKS):
        ct[core, zy] = masked[first:first + n]

    pl.semaphore_wait(barrier, len(GATHER) + len(PEERS) + 1)

    sends, y_sends, z_sends = [], [None], [None]

    def across_y(k):
        copy = pltpu.make_async_remote_copy(
            src_ref=cts[k].at[core, zy], dst_ref=cts[k].at[core, zy],
            send_sem=y_send.at[k - 1], recv_sem=y_recv.at[k - 1],
            device_id=gather_peer(1, 0, 1), device_id_type=MESH,
        )
        copy.start()
        y_sends.append(copy)

    across_y(1)
    for i, (oy, dz) in enumerate(GATHER):
        copy = pltpu.make_async_remote_copy(
            src_ref=ct0.at[core, zy], dst_ref=ct0.at[core, zy],
            send_sem=g_send.at[i], recv_sem=g_recv.at[i],
            device_id=gather_peer(oy, dz, 1), device_id_type=MESH,
        )
        copy.start()
        sends.append(copy)
    across_y(2)

    def along_z(k):
        y_sends[k].wait_recv()
        both = cts[k].at[core, pl.ds(z * 2, 2)]
        z_sends.append([])
        for i, dz in enumerate((2, 1, 3)):
            copy = pltpu.make_async_remote_copy(
                src_ref=both, dst_ref=both,
                send_sem=z_send.at[k - 1, i], recv_sem=z_recv.at[k - 1, i],
                device_id=gather_peer(0, dz, 1), device_id_type=MESH,
            )
            copy.start()
            z_sends[k].append(copy)

    def split_ints(g):
        loads[g].wait()

        def part(t, carry):
            at = pl.multiple_of(g * 256 + t * 64, 64)
            for p in range(PAIRS):
                hi, lo = split(ints[pl.ds(at * PAIRS + p, 64, stride=PAIRS), :])
                i_hi[pl.ds(at, 64), p * S:(p + 1) * S] = hi
                i_lo[pl.ds(at, 64), p * S:(p + 1) * S] = lo
            return carry

        lax.fori_loop(0, 4, part, 0)

    def forward(k):
        for copy in sends if k == 0 else z_sends[k]:
            copy.wait_recv()
        copy = pltpu.make_async_remote_copy(
            src_ref=cts[k].at[core], dst_ref=cts[k].at[core],
            send_sem=c_send.at[k], recv_sem=c_recv.at[k],
            device_id=sibling, device_id_type=MESH,
        )
        copy.start()
        return copy

    def assemble(k, copy, *places):
        copy.wait_recv()
        ct, n = cts[k], CHUNKS[k][1]
        for p in range(PAIRS):
            b = pair_ref[0, p]
            parts = split(ct[lax.rem(b, 2), b // 2])
            for lhs, *firsts in places:
                for first, part in zip(firsts, parts):
                    lhs[first:first + n, p * S:(p + 1) * S] = part

    def send(k, source, target, at, count):
        for dx, dy in PEERS:
            a = aux_peer(dx, dy)
            pltpu.make_async_remote_copy(
                src_ref=source(a, pl.ds(at, count)), dst_ref=target(pl.ds(aux * SHARE + at, count)),
                send_sem=a_send.at[k], recv_sem=a_recv.at[k],
                device_id=(blk, a), device_id_type=MESH,
            ).start()
        pltpu.make_async_copy(
            source(aux, pl.ds(at, count)), target(pl.ds(aux * SHARE + at, count)), a_recv.at[k]
        ).start()

    def send01(first, rows):
        o = pl.ds(first, rows)
        return functools.partial(
            send, 0, lambda a, at: half01.at[a, at, o], lambda at: recv01.at[at, o]
        )

    def send23(i):
        return functools.partial(
            send, 1 + i, lambda a, at: half23.at[i, a, at], lambda at: recv23.at[i, at]
        )

    def products(lhs, q, low, high, step):
        n = lhs.shape[0] // 2
        quarters = [q + r for r in range(n // QROWS)]

        def group(g, carry):
            at = pl.ds(pl.multiple_of(g * step * S, step * S), step * S)
            both = jnp.zeros((2 * n, step * S), f32)
            cross = jnp.zeros((n, step * S), f32)
            for j in range(K // 256):
                c = slice(j * 256, (j + 1) * 256)
                both += lax.dot_general(lhs[:, c], i_hi[at, c], NT, preferred_element_type=f32)
                cross += lax.dot_general(lhs[0:n, c], i_lo[at, c], NT, preferred_element_type=f32)
            total = both[:n] + (both[n:] + cross)
            for j in range(step):
                for i, r in enumerate(quarters):
                    rows = total[i * QROWS:(i + 1) * QROWS, j * S:(j + 1) * S].reshape(8, 8, S)
                    if r < 2:
                        half01[:, g * step + j, r * 8:r * 8 + 8] = rows
                    else:
                        half23[r - 2, :, g * step + j] = rows
            if q < 2:
                send01(q * 8, 8 * len(quarters))(g * step, step)
            else:
                send23(0)(g * step, step)
            return carry

        lax.fori_loop(low // step, high // step, group, 0)

    inputs[2].wait()
    metric = split(metric_ref[...])

    def arrived(k, buffer):
        pltpu.make_async_copy(buffer, buffer, a_recv.at[k]).wait()

    def finish(buffer, first):
        n = buffer.shape[1]
        flat = buffer.reshape(NAUX * n, S)
        parts = [flat[pl.ds(first + t, NAUX, stride=n), :] for t in range(8)]
        fitted = dot3(metric, split(jnp.concatenate(parts, axis=1)))
        fitted = jnp.concatenate([fitted[:, t * S:(t + 1) * S] for t in range(8)], axis=0)
        turned = jnp.concatenate([v.T for v in parts], axis=1)
        return dot3(split(turned), split(fitted))

    for g in range(4):
        split_ints(g)
    along_z(1)
    split_ints(4)
    f0 = forward(0)
    for g in range(5, NGROUPS):
        split_ints(g)
    along_z(2)
    assemble(0, f0, (lhs0, 0, QROWS), (lhs01, 0, 2 * QROWS))
    products(lhs0, 0, 0, 4, 2)
    f1 = forward(1)
    products(lhs0, 0, 4, 8, 4)
    assemble(1, f1, (lhs1, 0, QROWS), (lhs01, QROWS, 3 * QROWS))
    products(lhs01, 0, 8, SHARE, 2)
    products(lhs1, 1, 0, 4, 4)
    f2 = forward(2)
    products(lhs1, 1, 4, 8, 4)
    assemble(2, f2, (lhs2, 0, 2 * QROWS))
    products(lhs2, 2, 0, 8, 4)
    send23(1)(0, 8)
    products(lhs2, 2, 8, SHARE, 4)
    send23(1)(8, 8)
    arrived(0, recv01)
    band[...] = finish(recv01, 0)
    band[...] += finish(recv01, 8)
    for i in range(2):
        arrived(1 + i, recv23.at[i])
        band[...] += finish(recv23.at[i], 0)

    last = []
    for i, (dx, dy) in enumerate(PEERS):
        a = aux_peer(dx, dy)
        copy = pltpu.make_async_remote_copy(
            src_ref=band.at[pl.ds(pl.multiple_of(a * 16, 16), 16)], dst_ref=bands.at[i],
            send_sem=b_send.at[i], recv_sem=b_recv.at[i],
            device_id=(blk, a), device_id_type=MESH,
        )
        copy.start()
        last.append(copy)
    total = band[pl.ds(pl.multiple_of(aux * 16, 16), 16), :]
    for i, copy in enumerate(last):
        copy.wait_recv()
        total += bands[i]
    out_ref[...] = total

    for copy in sends + y_sends[1:] + z_sends[1] + z_sends[2] + [f0, f1, f2] + last:
        copy.wait_send()
    for k, sent in enumerate((half01.at[pl.ds(0, 7)], half23.at[0, pl.ds(0, 7)], half23.at[1, pl.ds(0, 7)])):
        pltpu.make_async_copy(sent, sent, a_send.at[k]).wait()


def local(coeffs, integrals, metric, pair_blocks, support):
    vmem = pl.BlockSpec(memory_space=pltpu.VMEM)
    dma = pltpu.SemaphoreType.DMA
    return pl.pallas_call(
        kernel,
        name="exchange",
        out_shape=jax.ShapeDtypeStruct((16, S), f32),
        in_specs=[pl.BlockSpec(memory_space=pltpu.SMEM)] + [pl.BlockSpec(memory_space=pl.ANY)] * 4,
        out_specs=vmem,
        scratch_shapes=[
            pltpu.VMEM((S, NOCC), f32),
            pltpu.VMEM((4, NOCC), jnp.int32),
            pltpu.VMEM((S, S), f32),
            pltpu.VMEM((SHARE * S * PAIRS, S), f32),
            pltpu.VMEM((SHARE * S, K), bf16),
            pltpu.VMEM((SHARE * S, K), bf16),
            *[pltpu.VMEM((2, 8, n, S), f32) for _, n in CHUNKS],
            *[pltpu.VMEM((2 * n, K), bf16) for n in (64, 64, 128, 128)],
            pltpu.VMEM((8, SHARE, 16, S), f32),
            pltpu.VMEM((2, 8, SHARE, 8, S), f32),
            pltpu.VMEM((NAUX, 16, S), f32),
            pltpu.VMEM((2, NAUX, 8, S), f32),
            pltpu.VMEM((S, S), f32),
            pltpu.VMEM((len(PEERS), 16, S), f32),
            dma((3,)),
            dma((NGROUPS,)),
            dma((len(GATHER),)),
            dma((len(GATHER),)),
            dma((2,)),
            dma((2,)),
            dma((2, 3)),
            dma((2, 3)),
            dma((3,)),
            dma((3,)),
            dma((3,)),
            dma((3,)),
            dma((len(PEERS),)),
            dma((len(PEERS),)),
        ],
        compiler_params=pltpu.CompilerParams(
            collective_id=0, has_side_effects=True, vmem_limit_bytes=56 * 2**20
        ),
    )(pair_blocks, coeffs, support.T, metric, integrals.reshape(SHARE * S * PAIRS, S))


def solution(mesh):
    return jax.shard_map(
        local,
        mesh=mesh,
        in_specs=(P("blk", None), P("blk", "aux", None, None, None), P(), P("blk", None), P()),
        out_specs=P(("blk", "aux"), None),
        check_vma=False,
    )
```

time: 269 us -> 51.6 us (0.19)
  waiting for transfers between devices: 162 us -> 0 us
  Pallas kernels: 0 us -> 50.1 us
  matrix products: 45.1 us -> 0 us
  blocking collectives: 29.9 us -> 0 us
  between operations: 13.5 us -> 0.01 us
  other arithmetic: 10.6 us -> 0 us
  local copies, waits for them, and re-layouts: 5.38 us -> 1.3 us
    ppermute x15 -> x0, waiting for transfers between devices: 97.6 us -> none  [from_behind(): return lax.ppermute(block, axis, route)]
    reduce_scatter x1 -> x0, waiting for transfers between devices: 64.4 us -> none  [local(): lax.psum_scatter(partial_band, 'aux', scatter_dimension=0, tiled=True)]
    pallas_call x0 -> x1, Pallas kernels: none -> 50.1 us  [local(): pl.pallas_call(kernel, name='exchange', out_shape=jax.ShapeDtypeStruct((1...]
    dot_general x3 -> x0, matrix products: 45.1 us -> none  [the longest x1 33.9 us: local(): jnp.einsum('bxk,bki->bxi', integrals.reshape(BLOCKS_DEV, share * S, PAIRS...]
    all_to_all x1 -> x0, blocking collectives: 29.9 us -> none  [local(): lax.all_to_all(half, 'aux', split_axis=3, concat_axis=1, tiled=True)]
    add x15 -> x0, other arithmetic: 7.01 us -> none  [pick(): collected + jnp.einsum('bpc,csi->bpsi', onehot, visiting, precision=hi)]
    another operation x1 -> x0, local copies, waits for them, and re-layouts: 3.12 us -> none
  transfers between devices with their start and end apart: 16 -> 0, of which waited for: 16 -> 0; matrix products, arithmetic and copies ran while one was open for 0% -> 0% of each run, Pallas kernels for 0% -> 0%
where the time goes in v1:
time: 51.6 us; the launch traced here: 51.4 us
  Pallas kernels  50.1 us (97%)
  local copies, waits for them, and re-layouts  1.3 us (3%)
    pallas_call x1, Pallas kernels, local(): pl.pallas_call(kernel, name='exchange', out_shape=jax.ShapeDtypeStruct((1...  50.1 us
    unnamed x1, local copies, waits for them, and re-layouts  1.3 us

profile of v1, /device:TPU:0, one launch (start us, length us, event | category | flops | bytes accessed | tf_op | source)
XLA Modules:
  0.0 51.4 jit_solution(16004684636088318465)
XLA Ops:
  0.0 50.1 %exchange.1 = f32[16,128]{1,0:T(8,128)} custom-call(s32[1,16]{1,0:T(1,128)} %pair_ref.1, f32[128,256]{1,0:T(8,128)} %coeffs_hbm.1, s32[4,256]{1,0:T(4,128)} %bitcast.3, f32[128,128]{1,0:T(8,128)} %metric_hbm.1, f32[32768,128]{1,0:T(8,128)} %bitcast.2), custom_call_target="tpu_custom_call" | custom-call | tf_op jit(solution)/shard_map/exchange/pallas_call | solution.py:284
  50.1 1.3 %copy.7 = f32[16,128]{1,0:T(8,128)} copy(f32[16,128]{1,0:T(8,128)} %exchange.1) | data formatting | bytes 16384

commit v2 on v1

--- a/solution.py
+++ b/solution.py
@@ -236,11 +236,11 @@
         split_ints(g)
     along_z(2)
     assemble(0, f0, (lhs0, 0, QROWS), (lhs01, 0, 2 * QROWS))
-    products(lhs0, 0, 0, 4, 2)
+    products(lhs0, 0, 0, 4, 4)
     f1 = forward(1)
     products(lhs0, 0, 4, 8, 4)
     assemble(1, f1, (lhs1, 0, QROWS), (lhs01, QROWS, 3 * QROWS))
-    products(lhs01, 0, 8, SHARE, 2)
+    products(lhs01, 0, 8, SHARE, 4)
     products(lhs1, 1, 0, 4, 4)
     f2 = forward(2)
     products(lhs1, 1, 4, 8, 4)

time: 51.6 us -> 51.5 us (level)
  no operation moved by 1% of the time
where the time goes in v2:
time: 51.5 us; the launch traced here: 51.4 us
  Pallas kernels  50.1 us (97%)
  local copies, waits for them, and re-layouts  1.3 us (3%)
    pallas_call x1, Pallas kernels, local(): pl.pallas_call(kernel, name='exchange', out_shape=jax.ShapeDtypeStruct((1...  50.1 us
    unnamed x1, local copies, waits for them, and re-layouts  1.3 us

profile of v2, /device:TPU:0, one launch (start us, length us, event | category | flops | bytes accessed | tf_op | source)
XLA Modules:
  0.0 51.4 jit_solution(12248694369283811751)
XLA Ops:
  0.0 50.1 %exchange.1 = f32[16,128]{1,0:T(8,128)} custom-call(s32[1,16]{1,0:T(1,128)} %pair_ref.1, f32[128,256]{1,0:T(8,128)} %coeffs_hbm.1, s32[4,256]{1,0:T(4,128)} %bitcast.3, f32[128,128]{1,0:T(8,128)} %metric_hbm.1, f32[32768,128]{1,0:T(8,128)} %bitcast.2), custom_call_target="tpu_custom_call" | custom-call | tf_op jit(solution)/shard_map/exchange/pallas_call | solution.py:284
  50.1 1.3 %copy.7 = f32[16,128]{1,0:T(8,128)} copy(f32[16,128]{1,0:T(8,128)} %exchange.1) | data formatting | bytes 16384

commit v3 on v2

--- a/solution.py
+++ b/solution.py
@@ -232,12 +232,13 @@
     along_z(1)
     split_ints(4)
     f0 = forward(0)
-    for g in range(5, NGROUPS):
-        split_ints(g)
+    split_ints(5)
     along_z(2)
     assemble(0, f0, (lhs0, 0, QROWS), (lhs01, 0, 2 * QROWS))
     products(lhs0, 0, 0, 4, 4)
     f1 = forward(1)
+    split_ints(6)
+    split_ints(7)
     products(lhs0, 0, 4, 8, 4)
     assemble(1, f1, (lhs1, 0, QROWS), (lhs01, QROWS, 3 * QROWS))
     products(lhs01, 0, 8, SHARE, 4)

time: 51.5 us -> 54.3 us (1.054)
  Pallas kernels: 50.1 us -> 52.8 us
    pallas_call x1, Pallas kernels: 50.1 us -> 52.8 us  [local(): pl.pallas_call(kernel, name='exchange', out_shape=jax.ShapeDtypeStruct((1...]
where the time goes in v3:
time: 54.3 us; the launch traced here: 54.1 us
  Pallas kernels  52.8 us (97%)
  local copies, waits for them, and re-layouts  1.3 us (2%)
    pallas_call x1, Pallas kernels, local(): pl.pallas_call(kernel, name='exchange', out_shape=jax.ShapeDtypeStruct((1...  52.8 us
    unnamed x1, local copies, waits for them, and re-layouts  1.3 us

profile of v3, /device:TPU:0, one launch (start us, length us, event | category | flops | bytes accessed | tf_op | source)
XLA Modules:
  0.0 54.1 jit_solution(5788566926642860083)
XLA Ops:
  0.0 52.8 %exchange.1 = f32[16,128]{1,0:T(8,128)} custom-call(s32[1,16]{1,0:T(1,128)} %pair_ref.1, f32[128,256]{1,0:T(8,128)} %coeffs_hbm.1, s32[4,256]{1,0:T(4,128)} %bitcast.3, f32[128,128]{1,0:T(8,128)} %metric_hbm.1, f32[32768,128]{1,0:T(8,128)} %bitcast.2), custom_call_target="tpu_custom_call" | custom-call | tf_op jit(solution)/shard_map/exchange/pallas_call | solution.py:285
  52.8 1.3 %copy.7 = f32[16,128]{1,0:T(8,128)} copy(f32[16,128]{1,0:T(8,128)} %exchange.1) | data formatting | bytes 16384

commit v4 on v2

--- a/solution.py
+++ b/solution.py
@@ -60,6 +60,13 @@
 
     sibling = (blk + 1 - 2 * core, aux)
 
+    barrier = pltpu.get_barrier_semaphore()
+    for oy, dz in GATHER:
+        pl.semaphore_signal(barrier, inc=1, device_id=gather_peer(oy, dz, -1), device_id_type=MESH)
+    for dx, dy in PEERS:
+        pl.semaphore_signal(barrier, inc=1, device_id=(blk, aux_peer(dx, dy)), device_id_type=MESH)
+    pl.semaphore_signal(barrier, inc=1, device_id=sibling, device_id_type=MESH)
+
     inputs = []
     for i, (src, dst) in enumerate(
         ((coeffs_hbm, coeffs_ref), (support_hbm, support_ref), (metric_hbm, metric_ref))
@@ -67,13 +74,6 @@
         load = pltpu.make_async_copy(src, dst, in_sem.at[i])
         load.start()
         inputs.append(load)
-    barrier = pltpu.get_barrier_semaphore()
-    for oy, dz in GATHER:
-        pl.semaphore_signal(barrier, inc=1, device_id=gather_peer(oy, dz, -1), device_id_type=MESH)
-    for dx, dy in PEERS:
-        pl.semaphore_signal(barrier, inc=1, device_id=(blk, aux_peer(dx, dy)), device_id_type=MESH)
-    pl.semaphore_signal(barrier, inc=1, device_id=sibling, device_id_type=MESH)
-
     inputs[0].wait()
     inputs[1].wait()
     loads = []

time: 51.5 us -> 51.5 us (level)
  no operation moved by 1% of the time
where the time goes in v4:
time: 51.5 us; the launch traced here: 51.4 us
  Pallas kernels  50.1 us (97%)
  local copies, waits for them, and re-layouts  1.3 us (3%)
    pallas_call x1, Pallas kernels, local(): pl.pallas_call(kernel, name='exchange', out_shape=jax.ShapeDtypeStruct((1...  50.1 us
    unnamed x1, local copies, waits for them, and re-layouts  1.3 us

profile of v4, /device:TPU:0, one launch (start us, length us, event | category | flops | bytes accessed | tf_op | source)
XLA Modules:
  0.0 51.4 jit_solution(7387956397331378276)
XLA Ops:
  0.0 50.1 %exchange.1 = f32[16,128]{1,0:T(8,128)} custom-call(s32[1,16]{1,0:T(1,128)} %pair_ref.1, f32[128,256]{1,0:T(8,128)} %coeffs_hbm.1, s32[4,256]{1,0:T(4,128)} %bitcast.3, f32[128,128]{1,0:T(8,128)} %metric_hbm.1, f32[32768,128]{1,0:T(8,128)} %bitcast.2), custom_call_target="tpu_custom_call" | custom-call | tf_op jit(solution)/shard_map/exchange/pallas_call | solution.py:284
  50.1 1.3 %copy.7 = f32[16,128]{1,0:T(8,128)} copy(f32[16,128]{1,0:T(8,128)} %exchange.1) | data formatting | bytes 16384
